TPU v7x, 32 devices: a whole 2x2x4 slice. The times are simulated.
32 devices in a mesh: replica: 2 (over x), patch: 8 (over z, y), band: 2 (over core).
Axes of the slice: x: 2, y: 2, z: 4, core: 2. Of those that a mesh axis runs over, the one named last changes fastest.
Arguments:
- grid_latent: bfloat16 [32768, 512], P(('replica', 'patch', 'band')), parts along dimension 0, may hold values from -6 to 6
- mesh_latent: bfloat16 [8192, 512], P(('replica', 'patch', 'band')), parts along dimension 0, may hold values from -6 to 6
- edge_features: bfloat16 [4, 32768], P(None, ('replica', 'patch', 'band')), parts along dimension 1, may hold values from -6 to 6
- edge_sender: int32 [32768], P(('replica', 'patch', 'band')), parts along dimension 0, may hold values from 0 to 1023
- edge_receiver: int32 [32768], P(('replica', 'patch', 'band')), parts along dimension 0, may hold values from 0 to 255
- block_offset: int32 [256], P(('replica', 'patch', 'band')), parts along dimension 0, may hold values from -2 to 2, as said below
- link_latent: bfloat16 [32768, 512], P(('replica', 'patch', 'band')), parts along dimension 0, may hold values from -6 to 6
- link_sender: int32 [32768], P(('replica', 'patch', 'band')), parts along dimension 0, may hold values from 0 to 4095, as said below
- link_receiver: int32 [32768], P(('replica', 'patch', 'band')), parts along dimension 0, may hold values from 0 to 255
- feature_weight: bfloat16 [4, 512], replicated, may hold values from -3 to 3
- source_weight: bfloat16 [512, 512], replicated, may hold values from -0.25 to 0.25
- target_weight: bfloat16 [512, 512], replicated, may hold values from -0.25 to 0.25
- edge_weight: bfloat16 [512, 512], replicated, may hold values from -0.25 to 0.25
- edge_second: bfloat16 [512, 512], replicated, may hold values from -0.25 to 0.25
- node_first: bfloat16 [512, 512], replicated, may hold values from -0.25 to 0.25
- node_summed: bfloat16 [512, 512], replicated, may hold values from -0.25 to 0.25
- node_second: bfloat16 [512, 512], replicated, may hold values from -0.25 to 0.25
- link_weight: bfloat16 [512, 512], replicated, may hold values from -0.25 to 0.25
- link_source: bfloat16 [512, 512], replicated, may hold values from -0.25 to 0.25
- link_target: bfloat16 [512, 512], replicated, may hold values from -0.25 to 0.25
- link_second: bfloat16 [512, 512], replicated, may hold values from -0.25 to 0.25
- vertex_first: bfloat16 [512, 512], replicated, may hold values from -0.25 to 0.25
- vertex_summed: bfloat16 [512, 512], replicated, may hold values from -0.25 to 0.25
- vertex_second: bfloat16 [512, 512], replicated, may hold values from -0.25 to 0.25
Outputs:
- mesh_out: bfloat16 [8192, 512], P(('replica', 'patch', 'band')), parts along dimension 0
There are 2 independent parts, one for each index of `replica`. A program takes and returns all parts, laid end to end along the dimension named above; an argument that names none is the same for every part. Nothing has to cross between parts.
Inputs may be any that keep to these rules, and one draw needn't show every extreme that they name: `block_offset`: at most 3 blocks of one device name the same offset, and on every device some offset is named by exactly 3 blocks. `link_sender`: the sender of a mesh edge lies on a device at most 2 positions away, cyclically along patch+band, from the edge's device.
All inputs are finite; a program needn't handle non-finite values.
Results may differ from a plain program's by a relative error of at most 0.014.
Values may be sent and summed in bfloat16 or wider, within the bound.
A program may use at most 64 MiB of HBM per device.

v0:
```python
import jax
import jax.numpy as jnp
from jax import lax
from jax.sharding import PartitionSpec as P

REACH = 2
BLOCK = 128
CAP_BLOCKS = 3


EPSILON = 1e-05


def from_behind(value, axis, steps):
    count = lax.axis_size(axis)
    pairs = [(source, (source + steps) % count) for source in range(count)]
    return lax.ppermute(value, axis, pairs)


def normalize(values):
    average = jnp.mean(values, axis=-1, keepdims=True)
    centred = values - average
    spread = jnp.mean(centred * centred, axis=-1, keepdims=True)
    return centred * lax.rsqrt(spread + EPSILON)


def project(left, right):
    return jnp.dot(left, right, preferred_element_type=jnp.float32)


def edge_update(base, before, second):
    hidden = jax.nn.silu(before).astype(jnp.bfloat16)
    return (base.astype(jnp.float32) + normalize(project(hidden, second))).astype(jnp.bfloat16)


def node_update(nodes, summed, first, summed_weight, second):
    before = project(nodes, first) + project(summed.astype(jnp.bfloat16), summed_weight)
    hidden = jax.nn.silu(before).astype(jnp.bfloat16)
    return (nodes.astype(jnp.float32) + normalize(project(hidden, second))).astype(jnp.bfloat16)


def embed_edges(features, weight):
    return lax.dot_general(
        features, weight, (((0,), (0,)), ((), ())), preferred_element_type=jnp.float32
    ).astype(jnp.bfloat16)


def node_totals(targets, updated, count):
    totals = jax.ops.segment_sum(updated.astype(jnp.float32), targets, count + 1)
    return totals[:count]


def body(
    grid_latent,
    mesh_latent,
    edge_features,
    edge_sender,
    edge_receiver,
    block_offset,
    link_latent,
    link_sender,
    link_receiver,
    feature_weight,
    source_weight,
    target_weight,
    edge_weight,
    edge_second,
    node_first,
    node_summed,
    node_second,
    link_weight,
    link_source,
    link_target,
    link_second,
    vertex_first,
    vertex_summed,
    vertex_second,
):
    mesh_rows = mesh_latent.shape[0]
    width = mesh_latent.shape[1]
    block_count = edge_sender.shape[0] // BLOCK
    offset_count = 2 * REACH + 1
    source_proj = project(grid_latent, source_weight).astype(jnp.bfloat16)
    target_proj = project(mesh_latent, target_weight).astype(jnp.bfloat16)
    shifted = block_offset + REACH
    matches = (shifted[:, None] == jnp.arange(offset_count, dtype=jnp.int32)[None, :]).astype(
        jnp.int32
    )
    position = jnp.sum(jnp.cumsum(matches, axis=0) * matches, axis=1) - 1
    slot_match = (
        shifted[None, None, :] == jnp.arange(offset_count, dtype=jnp.int32)[:, None, None]
    ) & (position[None, None, :] == jnp.arange(CAP_BLOCKS, dtype=jnp.int32)[None, :, None])
    source_block = jnp.sum(
        jnp.where(slot_match, jnp.arange(block_count, dtype=jnp.int32)[None, None, :], 0), axis=2
    )
    filled = jnp.any(slot_match, axis=2)
    edge_rows = source_proj[edge_sender].reshape(block_count, BLOCK, width)[source_block]
    packed_features = edge_features.reshape(edge_features.shape[0], block_count, BLOCK)[
        :, source_block
    ]
    packed_targets = jnp.where(
        filled[:, :, None], edge_receiver.reshape(block_count, BLOCK)[source_block], mesh_rows
    )
    arrived_rows = []
    arrived_features = []
    arrived_targets = []
    for offset_index in range(offset_count):
        shift_by = offset_index - REACH
        parcel = (
            edge_rows[offset_index].reshape(CAP_BLOCKS * BLOCK, width),
            packed_features[:, offset_index].reshape(edge_features.shape[0], CAP_BLOCKS * BLOCK),
            packed_targets[offset_index].reshape(CAP_BLOCKS * BLOCK),
        )
        if shift_by != 0:
            parcel = from_behind((parcel[0], parcel[1], parcel[2]), ("patch", "band"), shift_by)
        arrived_rows.append(parcel[0])
        arrived_features.append(parcel[1])
        arrived_targets.append(parcel[2])
    all_rows = jnp.concatenate(arrived_rows, axis=0)
    all_features = jnp.concatenate(arrived_features, axis=1)
    all_targets = jnp.concatenate(arrived_targets, axis=0)
    embedded = embed_edges(all_features, feature_weight)
    lookup = jnp.minimum(all_targets, mesh_rows - 1)
    before = (
        project(embedded, edge_weight)
        + all_rows.astype(jnp.float32)
        + target_proj[lookup].astype(jnp.float32)
    )
    updated = edge_update(embedded, before, edge_second)
    summed = node_totals(all_targets, updated, mesh_rows)
    mesh_next = node_update(mesh_latent, summed, node_first, node_summed, node_second)
    link_src = project(mesh_next, link_source).astype(jnp.bfloat16)
    link_dst = project(mesh_next, link_target).astype(jnp.bfloat16)
    group_size = lax.axis_size(("patch", "band"))
    position_here = lax.axis_index(("patch", "band"))
    source_tables = []
    for offset_index in range(offset_count):
        shift_by = offset_index - REACH
        if shift_by == 0:
            source_tables.append(link_src)
        else:
            source_tables.append(from_behind(link_src, ("patch", "band"), -shift_by))
    source_table = jnp.concatenate(source_tables, axis=0)
    owner = link_sender // mesh_rows
    owner_slot = (owner - position_here + REACH + group_size) % group_size
    sender_rows = source_table[owner_slot * mesh_rows + link_sender % mesh_rows]
    before = (
        project(link_latent, link_weight)
        + sender_rows.astype(jnp.float32)
        + link_dst[link_receiver].astype(jnp.float32)
    )
    link_new = edge_update(link_latent, before, link_second)
    link_sum = node_totals(link_receiver, link_new, mesh_rows)
    return node_update(mesh_next, link_sum, vertex_first, vertex_summed, vertex_second)


def solution(mesh):
    placed = (
        P(("replica", "patch", "band"), None),
        P(("replica", "patch", "band"), None),
        P(None, ("replica", "patch", "band")),
        P(("replica", "patch", "band")),
        P(("replica", "patch", "band")),
        P(("replica", "patch", "band")),
        P(("replica", "patch", "band"), None),
        P(("replica", "patch", "band")),
        P(("replica", "patch", "band")),
        P(),
        P(),
        P(),
        P(),
        P(),
        P(),
        P(),
        P(),
        P(),
        P(),
        P(),
        P(),
        P(),
        P(),
        P(),
    )
    return jax.shard_map(
        body,
        mesh=mesh,
        in_specs=placed,
        out_specs=P(("replica", "patch", "band"), None),
        check_vma=False,
    )
```

profile of v0, /device:TPU:0, one launch (start us, length us, event | category | flops | bytes accessed | tf_op | source)
XLA Modules:
  0.0 148.4 jit_solution(11936382425451313144)
XLA Ops:
  0.0 0.7 broadcast_add_fusion.1
  1.7 0.7 fusion.21
  2.4 1.2 gather_fusion
  3.7 6.1 %collective-permute-start = (s32[384]{0:T(512)S(1)}, s32[384]{0:T(512)S(1)}, u32[]{:S(2)}, u32[]{:S(2)}) collective-permute-start(s32[384]{0:T(512)S(1)} %get-tuple-element.18), channel_id=1, source_target_pairs={{0,14},{1,15},{2,0},{3,1},{4,2},{5,3},{6,4},{7,5},{8,6},{9,7},{10,... | collective-permute-start | bytes 4616 | tf_op jit(solution)/shard_map/ppermute | solution.py:17
  9.8 0.5 collective-permute-start.2
  10.3 0.7 collective-permute-start.3
  11.0 1.7 %convolution_convert_fusion.1 = bf16[1024,512]{1,0:T(8,128)(2,1)S(1)} fusion(bf16[1024,512]{1,0:T(8,128)(2,1)S(1)} %copy-done, bf16[512,512]{1,0:T(8,128)(2,1)} %param.34), kind=kOutput, calls=%fused_computation.21 | convolution fusion | flops 537395200 | bytes 2621440 | tf_op jit(solution)/shard_map/dot_general | solution.py:28
  12.8 4.0 %gather_fusion.2 = bf16[1024,512]{1,0:T(8,128)(2,1)S(1)} fusion(bf16[1024,512]{1,0:T(8,128)(2,1)S(1)} %convolution_convert_fusion.1, s32[1024]{0:T(1024)S(1)} %get-tuple-element.27), kind=kCustom, calls=%fused_computation.2 | custom fusion | bytes 2101248 | tf_op jit(solution)/shard_map/gather | solution.py:97
  16.7 2.0 %gather_fusion.3 = bf16[15,128,512]{2,1,0:T(8,128)(2,1)} fusion(bf16[8,128,512]{2,1,0:T(8,128)(2,1)S(1)} %bitcast.66, s32[1024]{0:T(1024)S(1)} %get-tuple-element.28), kind=kCustom, calls=%fused_computation.3 | custom fusion | bytes 3932220 | tf_op jit(solution)/shard_map/gather | solution.py:97
  18.7 2.9 %fusion.30 = (bf16[3,128,512]{2,1,0:T(8,128)(2,1)}, bf16[3,128,512]{2,1,0:T(8,128)(2,1)}, bf16[3,128,512]{2,1,0:T(8,128)(2,1)}, bf16[3,128,512]{2,1,0:T(8,128)(2,1)}, bf16[3,128,512]{2,1,0:T(8,128)(2,1)}) fusion(bf16[15,128,512]{2,1,0:T(8,128)(2,1)} %gather_fusion.3), kind=kLoop, calls=%fused_computation.128 | loop fusion | bytes 3932160 | tf_op jit(solution)/shard_map/slice | solution.py:110
  21.6 4.1 %collective-permute-start.8 = (bf16[384,512]{1,0:T(8,128)(2,1)}, bf16[384,512]{1,0:T(8,128)(2,1)}, u32[]{:S(2)}, u32[]{:S(2)}) collective-permute-start(bf16[384,512]{1,0:T(8,128)(2,1)} %bitcast.17), channel_id=1, source_target_pairs={{0,14},{1,15},{2,0},{3,1},{4,2},{5,3},{6,4},{7,5},{8,6},{9,7},{10,... | collective-permute-start | bytes 1179656 | tf_op jit(solution)/shard_map/ppermute | solution.py:17
  25.6 0.6 gather_fusion.1
  26.5 2.2 %fusion.39 = f32[256,512]{1,0:T(8,128)} fusion(bf16[256,512]{1,0:T(8,128)(2,1)S(1)} %copy-done.2, bf16[512,512]{1,0:T(8,128)(2,1)} %param.38), kind=kOutput, calls=%fused_computation.135 | convolution fusion | flops 134217728 | bytes 1310720 | tf_op jit(solution)/shard_map/dot_general | solution.py:28
  28.8 1.4 copy.35
  30.2 0.7 collective-permute-start.9
  30.9 1.2 collective-permute-start.11
  32.2 3.5 %collective-permute-start.4 = (bf16[4,384]{1,0:T(4,128)(2,1)S(1)}, bf16[4,384]{1,0:T(4,128)(2,1)S(1)}, u32[]{:S(2)}, u32[]{:S(2)}) collective-permute-start(bf16[4,384]{1,0:T(4,128)(2,1)S(1)} %get-tuple-element.13), channel_id=1, source_target_pairs={{0,14},{1,15},{2,0},{3,1},{4,2},{5,3},{6,4},{7,5},{8,6},{9,7},{10,... | collective-permute-start | bytes 9224 | tf_op jit(solution)/shard_map/ppermute | solution.py:17
  35.9 6.8 %gather_fusion.4 = bf16[1920,512]{1,0:T(8,128)(2,1)} fusion(bf16[256,512]{1,0:T(8,128)(2,1)S(1)} %convolution_convert_fusion.4, s32[2048]{0:T(1024)S(1)} %pad_clamp_fusion), kind=kCustom, calls=%fused_computation.4 | custom fusion | bytes 3939840 | tf_op jit(solution)/shard_map/gather | solution.py:127
  42.6 8.1 %collective-permute-done.4 = bf16[4,384]{1,0:T(4,128)(2,1)S(1)} collective-permute-done((bf16[4,384]{1,0:T(4,128)(2,1)S(1)}, bf16[4,384]{1,0:T(4,128)(2,1)S(1)}, u32[]{:S(2)}, u32[]{:S(2)}) %collective-permute-start.4) | collective-permute-done | bytes 3104 | tf_op jit(solution)/shard_map/ppermute | solution.py:17
  50.7 1.3 collective-permute-done.5
  52.1 5.7 %collective-permute-done.6 = bf16[4,384]{1,0:T(4,128)(2,1)S(1)} collective-permute-done((bf16[4,384]{1,0:T(4,128)(2,1)S(1)}, bf16[4,384]{1,0:T(4,128)(2,1)S(1)}, u32[]{:S(2)}, u32[]{:S(2)}) %collective-permute-start.6) | collective-permute-done | bytes 3104 | tf_op jit(solution)/shard_map/ppermute | solution.py:17
  57.8 6.3 %collective-permute-done.7 = bf16[4,384]{1,0:T(4,128)(2,1)S(1)} collective-permute-done((bf16[4,384]{1,0:T(4,128)(2,1)S(1)}, bf16[4,384]{1,0:T(4,128)(2,1)S(1)}, u32[]{:S(2)}, u32[]{:S(2)}) %collective-permute-start.7) | collective-permute-done | bytes 3104 | tf_op jit(solution)/shard_map/ppermute | solution.py:17
  64.1 0.7 convolution_convert_fusion
  64.8 1.8 %constant_dynamic-update-slice_fusion.10 = bf16[1920,512]{1,0:T(8,128)(2,1)} fusion(bf16[384,512]{1,0:T(8,128)(2,1)} %collective-permute-done.8), kind=kLoop, calls=%fused_computation.55 | loop fusion | bytes 786432
  66.6 1.8 %constant_dynamic-update-slice_fusion.9 = bf16[1920,512]{1,0:T(8,128)(2,1)} fusion(bf16[1920,512]{1,0:T(8,128)(2,1)} %constant_dynamic-update-slice_fusion.10, bf16[384,512]{1,0:T(8,128)(2,1)} %collective-permute-done.9), kind=kLoop, calls=%fused_computation.54 | loop fusion | bytes 786432
  68.4 0.8 constant_dynamic-update-slice_fusion.8
  69.2 1.8 %constant_dynamic-update-slice_fusion.7 = bf16[1920,512]{1,0:T(8,128)(2,1)} fusion(bf16[1920,512]{1,0:T(8,128)(2,1)} %constant_dynamic-update-slice_fusion.8, bf16[384,512]{1,0:T(8,128)(2,1)} %collective-permute-done.10), kind=kLoop, calls=%fused_computation.52 | loop fusion | bytes 786432
  71.0 1.8 %constant_dynamic-update-slice_fusion.6 = bf16[1920,512]{1,0:T(8,128)(2,1)} fusion(bf16[1920,512]{1,0:T(8,128)(2,1)} %constant_dynamic-update-slice_fusion.7, bf16[384,512]{1,0:T(8,128)(2,1)} %collective-permute-done.11), kind=kLoop, calls=%fused_computation.51 | loop fusion | bytes 786432 | tf_op jit(solution)/shard_map/concatenate | solution.py:119
  72.7 7.1 %fusion.31 = (f32[1920]{0:T(1024)S(1)}, f32[1920,512]{0,1:T(8,128)}) fusion(bf16[512,512]{1,0:T(8,128)(2,1)} %param.37, bf16[1920,512]{1,0:T(8,128)(2,1)} %gather_fusion.4, bf16[1920,512]{1,0:T(8,128)(2,1)} %constant_dynamic-update-slice_fusion.6, bf16[1920,512]{1,0:T(8,128)(2,1)S(1)} %convolution_convert_fusion, bf16[512,512]{1,0:T(8,128)(2,1)} %param.36), kind=kOutput, calls=%fused_computation.129 | convolution fusion | flops 2023094400 | bytes 10886656 | tf_op jit(solution)/shard_map/dot_general | solution.py:28
  79.8 5.4 %copy.34 = f32[1920,512]{1,0:T(8,128)} copy(f32[1920,512]{0,1:T(8,128)} %get-tuple-element.20) | data formatting | bytes 7864320 | tf_op jit(solution)/shard_map/dot_general | solution.py:28
  85.3 2.8 %multiply_reduce_fusion = f32[1920]{0:T(1024)S(1)} fusion(f32[1920,512]{1,0:T(8,128)} %copy.34, f32[1920]{0:T(1024)S(1)} %broadcast_multiply_fusion), kind=kLoop, calls=%fused_computation.12 | loop fusion | flops 2947200 | bytes 3947520 | tf_op jit(solution)/shard_map/reduce_sum | solution.py:23
  88.1 16.4 %scatter_custom_fusion = f32[257,512]{1,0:T(8,128)} fusion(s32[1920]{0:T(1024)S(1)} %constant_dynamic-update-slice_fusion.22, bf16[1920,512]{1,0:T(8,128)(2,1)S(1)} %convolution_convert_fusion, f32[1920,512]{1,0:T(8,128)} %copy.34, f32[1920]{0:T(1024)S(1)} %add_rsqrt_fusion, f32[1920]{0:T(1024)S(1)} %broadcast_multiply_fusion, f32[]{:T(128)} %constant.82.clone.1), kind=kCustom, calls=%fused_computation.9 | custom fusion | flops 6881280 | bytes 6440964 | tf_op jit(solution)/shard_map/scatter-add | solution.py:49
  104.5 2.2 %fusion.32 = (f32[256]{0:T(256)S(1)}, f32[256,512]{1,0:T(8,128)S(1)}) fusion(bf16[512,512]{1,0:T(8,128)(2,1)} %param.40, f32[256,512]{1,0:T(8,128)} %fusion.39, bf16[512,512]{1,0:T(8,128)(2,1)} %param.39, f32[257,512]{1,0:T(8,128)} %scatter_custom_fusion), kind=kOutput, calls=%fused_computation.130 | convolution fusion | flops 269352704 | bytes 2360320 | tf_op jit(solution)/shard_map/dot_general | solution.py:28
  107.6 4.4 %collective-permute-start.14 = (bf16[256,512]{1,0:T(8,128)(2,1)S(1)}, bf16[256,512]{1,0:T(8,128)(2,1)S(1)}, u32[]{:S(2)}, u32[]{:S(2)}) collective-permute-start(bf16[256,512]{1,0:T(8,128)(2,1)S(1)} %convolution_convert_fusion.3), channel_id=1, source_target_pairs={{0,15},{1,0},{2,1},{3,2},{4,3},{5,4},{6,5},{7,6},{8,7},{9,8},{10,9... | collective-permute-start | bytes 786440 | tf_op jit(solution)/shard_map/ppermute | solution.py:17
  112.0 2.0 %collective-permute-start.15 = (bf16[256,512]{1,0:T(8,128)(2,1)S(1)}, bf16[256,512]{1,0:T(8,128)(2,1)S(1)}, u32[]{:S(2)}, u32[]{:S(2)}) collective-permute-start(bf16[256,512]{1,0:T(8,128)(2,1)S(1)} %convolution_convert_fusion.3), channel_id=1, source_target_pairs={{0,14},{1,15},{2,0},{3,1},{4,2},{5,3},{6,4},{7,5},{8,6},{9,7},{10,... | collective-permute-start | bytes 786440 | tf_op jit(solution)/shard_map/ppermute | solution.py:17
  114.3 5.1 %gather_fusion.6 = bf16[1024,512]{1,0:T(8,128)(2,1)} fusion(bf16[256,512]{1,0:T(8,128)(2,1)S(1)} %convolution_convert_fusion.2, s32[1024]{0:T(1024)S(1)} %get-tuple-element.30), kind=kCustom, calls=%fused_computation.6 | custom fusion | bytes 2101248 | tf_op jit(solution)/shard_map/gather | solution.py:150
  119.4 1.1 fusion.40
  120.5 1.0 constant_dynamic-update-slice_fusion.20
  121.4 1.0 constant_dynamic-update-slice_fusion.19
  122.5 1.6 %collective-permute-done.15 = bf16[256,512]{1,0:T(8,128)(2,1)S(1)} collective-permute-done((bf16[256,512]{1,0:T(8,128)(2,1)S(1)}, bf16[256,512]{1,0:T(8,128)(2,1)S(1)}, u32[]{:S(2)}, u32[]{:S(2)}) %collective-permute-start.15) | collective-permute-done | bytes 262176 | tf_op jit(solution)/shard_map/ppermute | solution.py:17
  124.1 5.1 %gather_fusion.5 = bf16[1024,512]{1,0:T(8,128)(2,1)} fusion(bf16[1280,512]{1,0:T(8,128)(2,1)S(1)} %constant_dynamic-update-slice_fusion.16, s32[1024]{0:T(1024)S(1)} %get-tuple-element.29), kind=kCustom, calls=%fused_computation.5 | custom fusion | bytes 2101248 | tf_op jit(solution)/shard_map/gather | solution.py:146
  129.2 3.8 %fusion.33 = (f32[1024]{0:T(1024)S(1)}, f32[1024,512]{0,1:T(8,128)S(1)}) fusion(bf16[512,512]{1,0:T(8,128)(2,1)} %param.44, bf16[1024,512]{1,0:T(8,128)(2,1)} %gather_fusion.6, bf16[1024,512]{1,0:T(8,128)(2,1)} %gather_fusion.5, bf16[1024,512]{1,0:T(8,128)(2,1)} %param.30, bf16[512,512]{1,0:T(8,128)(2,1)} %param.41), kind=kOutput, calls=%fused_computation.131 | convolution fusion | flops 1078983680 | bytes 6295552 | tf_op jit(solution)/shard_map/dot_general | solution.py:28
  133.2 0.9 copy-done.1
  134.1 1.7 %fusion.5 = f32[1024,512]{0,1:T(8,128)} fusion(f32[1024,512]{0,1:T(8,128)S(1)} %get-tuple-element.24, bf16[1024,512]{0,1:T(8,128)(2,1)S(1)} %copy-done.1, f32[1024]{0:T(1024)S(1)} %add_rsqrt_fusion.1, f32[1024]{0:T(1024)S(1)} %broadcast_multiply_fusion.1), kind=kLoop, calls=%fused_computation.27 | loop fusion | flops 3145728 | bytes 5251072 | tf_op jit(solution)/shard_map/convert_element_type | solution.py:49
  135.9 1.9 %copy.36 = f32[1024,512]{1,0:T(8,128)S(1)} copy(f32[1024,512]{0,1:T(8,128)} %fusion.5) | data formatting | bytes 4194304 | tf_op jit(solution)/shard_map/convert_element_type | solution.py:49
  137.8 7.4 %scatter_custom_fusion.1 = f32[257,512]{1,0:T(8,128)} fusion(s32[1024]{0:T(1024)S(1)} %copy-done.12, f32[1024,512]{1,0:T(8,128)S(1)} %copy.36, f32[]{:T(128)} %constant.82.clone.1), kind=kCustom, calls=%fused_computation.39 | custom fusion | flops 524288 | bytes 526340 | tf_op jit(solution)/shard_map/scatter-add | solution.py:49
  145.2 2.2 %fusion.34 = (f32[256]{0:T(256)S(1)}, f32[256,512]{1,0:T(8,128)S(1)}) fusion(bf16[512,512]{1,0:T(8,128)(2,1)} %param.47, f32[256,512]{1,0:T(8,128)} %fusion.40, bf16[512,512]{1,0:T(8,128)(2,1)} %param.46, f32[257,512]{1,0:T(8,128)} %scatter_custom_fusion.1), kind=kOutput, calls=%fused_computation.132 | convolution fusion | flops 269352704 | bytes 2360320 | tf_op jit(solution)/shard_map/dot_general | solution.py:28
  147.6 0.9 add_convert_fusion.3
  (96 shorter events, 3.3 us)
Async XLA Ops:
  0.0 11.0 %copy-start = (bf16[1024,512]{1,0:T(8,128)(2,1)S(1)}, bf16[1024,512]{1,0:T(8,128)(2,1)}, u32[]{:S(2)}) copy-start(bf16[1024,512]{1,0:T(8,128)(2,1)} %param.24) | copy-start | bytes 3145732
  3.7 26.5 %collective-permute-start = (s32[384]{0:T(512)S(1)}, s32[384]{0:T(512)S(1)}, u32[]{:S(2)}, u32[]{:S(2)}) collective-permute-start(s32[384]{0:T(512)S(1)} %get-tuple-element.18), channel_id=1, source_target_pairs={{0,14},{1,15},{2,0},{3,1},{4,2},{5,3},{6,4},{7,5},{8,6},{9,7},{10,... | collective-permute-start | bytes 4616 | tf_op jit(solution)/shard_map/ppermute | solution.py:17
  9.8 21.1 %collective-permute-start.1 = (s32[384]{0:T(512)S(1)}, s32[384]{0:T(512)S(1)}, u32[]{:S(2)}, u32[]{:S(2)}) collective-permute-start(s32[384]{0:T(512)S(1)} %get-tuple-element.17), channel_id=1, source_target_pairs={{0,15},{1,0},{2,1},{3,2},{4,3},{5,4},{6,5},{7,6},{8,7},{9,8},{10,9... | collective-permute-start | bytes 4616 | tf_op jit(solution)/shard_map/ppermute | solution.py:17
  9.8 21.1 %collective-permute-start.2 = (s32[384]{0:T(512)S(1)}, s32[384]{0:T(512)S(1)}, u32[]{:S(2)}, u32[]{:S(2)}) collective-permute-start(s32[384]{0:T(512)S(1)} %get-tuple-element.16), channel_id=1, source_target_pairs={{0,1},{1,2},{2,3},{3,4},{4,5},{5,6},{6,7},{7,8},{8,9},{9,10},{10,1... | collective-permute-start | bytes 4616 | tf_op jit(solution)/shard_map/ppermute | solution.py:17
  10.3 21.9 %collective-permute-start.3 = (s32[384]{0:T(512)S(1)}, s32[384]{0:T(512)S(1)}, u32[]{:S(2)}, u32[]{:S(2)}) collective-permute-start(s32[384]{0:T(512)S(1)} %get-tuple-element.15), channel_id=1, source_target_pairs={{0,2},{1,3},{2,4},{3,5},{4,6},{5,7},{6,8},{7,9},{8,10},{9,11},{10,... | collective-permute-start | bytes 4616 | tf_op jit(solution)/shard_map/ppermute | solution.py:17
  18.7 6.9 %copy-start.9 = (bf16[4,1024]{1,0:T(4,128)(2,1)S(1)}, bf16[4,1024]{1,0:T(4,128)(2,1)}, u32[]{:S(2)}) copy-start(bf16[4,1024]{1,0:T(4,128)(2,1)} %param.26) | copy-start | bytes 24580
  18.7 7.5 %copy-start.2 = (bf16[256,512]{1,0:T(8,128)(2,1)S(1)}, bf16[256,512]{1,0:T(8,128)(2,1)}, u32[]{:S(2)}) copy-start(bf16[256,512]{1,0:T(8,128)(2,1)} %param.25) | copy-start | bytes 786436
  18.7 7.5 %copy-start.5 = (bf16[512,512]{1,0:T(8,128)(2,1)S(1)}, bf16[512,512]{1,0:T(8,128)(2,1)}, u32[]{:S(2)}) copy-start(bf16[512,512]{1,0:T(8,128)(2,1)} %param.35) | copy-start | bytes 1572868
  21.6 7.2 %copy-start.11 = (s32[1024]{0:T(1024)S(1)}, s32[1024]{0:T(1024)}, u32[]{:S(2)}) copy-start(s32[1024]{0:T(1024)} %param.31) | copy-start | bytes 12292
  21.6 7.2 %copy-start.12 = (s32[1024]{0:T(1024)S(1)}, s32[1024]{0:T(1024)}, u32[]{:S(2)}) copy-start(s32[1024]{0:T(1024)} %param.32) | copy-start | bytes 12292
  21.6 7.3 %copy-start.4 = (bf16[1024,512]{1,0:T(8,128)(2,1)S(1)}, bf16[1024,512]{1,0:T(8,128)(2,1)}, u32[]{:S(2)}) copy-start(bf16[1024,512]{1,0:T(8,128)(2,1)} %param.30) | copy-start | bytes 3145732
  21.6 43.2 %collective-permute-start.8 = (bf16[384,512]{1,0:T(8,128)(2,1)}, bf16[384,512]{1,0:T(8,128)(2,1)}, u32[]{:S(2)}, u32[]{:S(2)}) collective-permute-start(bf16[384,512]{1,0:T(8,128)(2,1)} %bitcast.17), channel_id=1, source_target_pairs={{0,14},{1,15},{2,0},{3,1},{4,2},{5,3},{6,4},{7,5},{8,6},{9,7},{10,... | collective-permute-start | bytes 1179656 | tf_op jit(solution)/shard_map/ppermute | solution.py:17
  30.2 36.4 %collective-permute-start.9 = (bf16[384,512]{1,0:T(8,128)(2,1)}, bf16[384,512]{1,0:T(8,128)(2,1)}, u32[]{:S(2)}, u32[]{:S(2)}) collective-permute-start(bf16[384,512]{1,0:T(8,128)(2,1)} %bitcast.18), channel_id=1, source_target_pairs={{0,15},{1,0},{2,1},{3,2},{4,3},{5,4},{6,5},{7,6},{8,7},{9,8},{10,9... | collective-permute-start | bytes 1179656 | tf_op jit(solution)/shard_map/ppermute | solution.py:17
  30.9 38.3 %collective-permute-start.10 = (bf16[384,512]{1,0:T(8,128)(2,1)}, bf16[384,512]{1,0:T(8,128)(2,1)}, u32[]{:S(2)}, u32[]{:S(2)}) collective-permute-start(bf16[384,512]{1,0:T(8,128)(2,1)} %bitcast.20), channel_id=1, source_target_pairs={{0,1},{1,2},{2,3},{3,4},{4,5},{5,6},{6,7},{7,8},{8,9},{9,10},{10,1... | collective-permute-start | bytes 1179656 | tf_op jit(solution)/shard_map/ppermute | solution.py:17
  30.9 40.0 %collective-permute-start.11 = (bf16[384,512]{1,0:T(8,128)(2,1)}, bf16[384,512]{1,0:T(8,128)(2,1)}, u32[]{:S(2)}, u32[]{:S(2)}) collective-permute-start(bf16[384,512]{1,0:T(8,128)(2,1)} %bitcast.21), channel_id=1, source_target_pairs={{0,2},{1,3},{2,4},{3,5},{4,6},{5,7},{6,8},{7,9},{8,10},{9,11},{10,... | collective-permute-start | bytes 1179656 | tf_op jit(solution)/shard_map/ppermute | solution.py:17
  32.2 18.6 %collective-permute-start.4 = (bf16[4,384]{1,0:T(4,128)(2,1)S(1)}, bf16[4,384]{1,0:T(4,128)(2,1)S(1)}, u32[]{:S(2)}, u32[]{:S(2)}) collective-permute-start(bf16[4,384]{1,0:T(4,128)(2,1)S(1)} %get-tuple-element.13), channel_id=1, source_target_pairs={{0,14},{1,15},{2,0},{3,1},{4,2},{5,3},{6,4},{7,5},{8,6},{9,7},{10,... | collective-permute-start | bytes 9224 | tf_op jit(solution)/shard_map/ppermute | solution.py:17
  35.8 28.2 %copy-start.10 = (bf16[4,512]{1,0:T(4,128)(2,1)S(1)}, bf16[4,512]{1,0:T(4,128)(2,1)}, u32[]{:S(2)}) copy-start(bf16[4,512]{1,0:T(4,128)(2,1)} %param.33) | copy-start | bytes 12292
  42.6 25.8 %copy-start.3 = (bf16[3,128,512]{2,1,0:T(8,128)(2,1)S(1)}, bf16[3,128,512]{2,1,0:T(8,128)(2,1)}, u32[]{:S(2)}) copy-start(bf16[3,128,512]{2,1,0:T(8,128)(2,1)} %get-tuple-element.7) | copy-start | bytes 1179652
  50.7 1.3 collective-permute-start.5
  52.1 5.7 %collective-permute-start.6 = (bf16[4,384]{1,0:T(4,128)(2,1)S(1)}, bf16[4,384]{1,0:T(4,128)(2,1)S(1)}, u32[]{:S(2)}, u32[]{:S(2)}) collective-permute-start(bf16[4,384]{1,0:T(4,128)(2,1)S(1)} %get-tuple-element.11), channel_id=1, source_target_pairs={{0,1},{1,2},{2,3},{3,4},{4,5},{5,6},{6,7},{7,8},{8,9},{9,10},{10,1... | collective-permute-start | bytes 9224 | tf_op jit(solution)/shard_map/ppermute | solution.py:17
  57.8 6.3 %collective-permute-start.7 = (bf16[4,384]{1,0:T(4,128)(2,1)S(1)}, bf16[4,384]{1,0:T(4,128)(2,1)S(1)}, u32[]{:S(2)}, u32[]{:S(2)}) collective-permute-start(bf16[4,384]{1,0:T(4,128)(2,1)S(1)} %get-tuple-element.10), channel_id=1, source_target_pairs={{0,2},{1,3},{2,4},{3,5},{4,6},{5,7},{6,8},{7,9},{8,10},{9,11},{10,... | collective-permute-start | bytes 9224 | tf_op jit(solution)/shard_map/ppermute | solution.py:17
  104.5 2.6 %copy-start.6 = (bf16[512,512]{1,0:T(8,128)(2,1)S(1)}, bf16[512,512]{1,0:T(8,128)(2,1)}, u32[]{:S(2)}) copy-start(bf16[512,512]{1,0:T(8,128)(2,1)} %param.42) | copy-start | bytes 1572868
  106.7 7.2 %copy-start.7 = (bf16[512,512]{1,0:T(8,128)(2,1)S(1)}, bf16[512,512]{1,0:T(8,128)(2,1)}, u32[]{:S(2)}) copy-start(bf16[512,512]{1,0:T(8,128)(2,1)} %param.43) | copy-start | bytes 1572868
  107.4 13.0 %collective-permute-start.12 = (bf16[256,512]{1,0:T(8,128)(2,1)S(1)}, bf16[256,512]{1,0:T(8,128)(2,1)}, u32[]{:S(2)}, u32[]{:S(2)}) collective-permute-start(bf16[256,512]{1,0:T(8,128)(2,1)S(1)} %convolution_convert_fusion.3), channel_id=1, source_target_pairs={{0,2},{1,3},{2,4},{3,5},{4,6},{5,7},{6,8},{7,9},{8,10},{9,11},{10,... | collective-permute-start | bytes 786440 | tf_op jit(solution)/shard_map/ppermute | solution.py:17
  107.5 13.9 %collective-permute-start.13 = (bf16[256,512]{1,0:T(8,128)(2,1)S(1)}, bf16[256,512]{1,0:T(8,128)(2,1)}, u32[]{:S(2)}, u32[]{:S(2)}) collective-permute-start(bf16[256,512]{1,0:T(8,128)(2,1)S(1)} %convolution_convert_fusion.3), channel_id=1, source_target_pairs={{0,1},{1,2},{2,3},{3,4},{4,5},{5,6},{6,7},{7,8},{8,9},{9,10},{10,1... | collective-permute-start | bytes 786440 | tf_op jit(solution)/shard_map/ppermute | solution.py:17
  107.6 14.9 %collective-permute-start.14 = (bf16[256,512]{1,0:T(8,128)(2,1)S(1)}, bf16[256,512]{1,0:T(8,128)(2,1)S(1)}, u32[]{:S(2)}, u32[]{:S(2)}) collective-permute-start(bf16[256,512]{1,0:T(8,128)(2,1)S(1)} %convolution_convert_fusion.3), channel_id=1, source_target_pairs={{0,15},{1,0},{2,1},{3,2},{4,3},{5,4},{6,5},{7,6},{8,7},{9,8},{10,9... | collective-permute-start | bytes 786440 | tf_op jit(solution)/shard_map/ppermute | solution.py:17
  112.0 12.1 %collective-permute-start.15 = (bf16[256,512]{1,0:T(8,128)(2,1)S(1)}, bf16[256,512]{1,0:T(8,128)(2,1)S(1)}, u32[]{:S(2)}, u32[]{:S(2)}) collective-permute-start(bf16[256,512]{1,0:T(8,128)(2,1)S(1)} %convolution_convert_fusion.3), channel_id=1, source_target_pairs={{0,14},{1,15},{2,0},{3,1},{4,2},{5,3},{6,4},{7,5},{8,6},{9,7},{10,... | collective-permute-start | bytes 786440 | tf_op jit(solution)/shard_map/ppermute | solution.py:17
  114.3 5.1 %copy-start.8 = (bf16[512,512]{1,0:T(8,128)(2,1)S(1)}, bf16[512,512]{1,0:T(8,128)(2,1)}, u32[]{:S(2)}) copy-start(bf16[512,512]{1,0:T(8,128)(2,1)} %param.45) | copy-start | bytes 1572868
  132.9 1.2 copy-start.1
where the time goes:
time: 149 us; the launch traced here: 148 us
  local copies, waits for them, and re-layouts  47.5 us (32%)
  other arithmetic  32.3 us (22%)
  starting transfers between devices  23.3 us (16%)
  waiting for transfers between devices  23 us (15%)
  matrix products  21.9 us (15%)
    scatter-add x2, other arithmetic, node_totals(): jax.ops.segment_sum(updated.astype(jnp.float32), targets, count + 1)  23.8 us
    ppermute x16, starting transfers between devices, from_behind(): return lax.ppermute(value, axis, pairs)  23.3 us
    ppermute x16, waiting for transfers between devices, from_behind(): return lax.ppermute(value, axis, pairs)  23 us
    dot_general x10, matrix products, project(): return jnp.dot(left, right, preferred_element_type=jnp.float32)  21.2 us
    unnamed x48, local copies, waits for them, and re-layouts  10.5 us
    gather x1, local copies, waits for them, and re-layouts, body(): target_proj[lookup].astype(jnp.float32)  6.78 us
    gather x2, local copies, waits for them, and re-layouts, body(): source_proj[edge_sender].reshape(block_count, BLOCK, width)[source_block]  5.93 us
    dot_general x1, local copies, waits for them, and re-layouts, project(): return jnp.dot(left, right, preferred_element_type=jnp.float32)  5.45 us
  transfers between devices with their start and end apart: 16, of which 5 were waited for; matrix products, arithmetic and copies ran while one was open for 25% of the time, Pallas kernels for 0%

commit v1 on v0

v1 whole, which is shorter than its diff:
```python
import functools

import jax
import jax.numpy as jnp
from jax import lax
from jax.experimental import pallas as pl
from jax.experimental.pallas import tpu as pltpu
from jax.sharding import PartitionSpec as P

REACH = 2
BLOCK = 128
EPSILON = 1e-05
CHUNKS = 2
TILE = 256
LANES = 128
AXES = ("replica", "patch", "band")
BF16 = jnp.bfloat16
F32 = jnp.float32

WEIGHTS = 14


def mm(left, right):
    return jnp.dot(left, right, preferred_element_type=F32)


def silu(value):
    half = 0.5 * value
    return half + half * jnp.tanh(half)


def normalize(values):
    average = jnp.mean(values, axis=-1, keepdims=True)
    centred = values - average
    spread = jnp.mean(centred * centred, axis=-1, keepdims=True)
    return centred * lax.rsqrt(spread + EPSILON)


def as_columns(row):
    return jnp.transpose(jnp.broadcast_to(row, (LANES, LANES)))


def one_hot_rows(keys, width):
    parts = []
    for at in range(keys.shape[1] // LANES):
        columns = as_columns(keys[:, at * LANES : (at + 1) * LANES])
        wide = jnp.concatenate([columns] * (width // LANES), axis=1)
        ids = lax.broadcasted_iota(jnp.int32, (LANES, width), 1)
        parts.append(jnp.where(wide == ids, 1.0, 0.0).astype(BF16))
    return jnp.concatenate(parts, axis=0)


def one_hot_columns(keys, first, height):
    ids = lax.broadcasted_iota(jnp.int32, (height, keys.shape[1]), 0)
    return jnp.where(jnp.broadcast_to(keys - first, ids.shape) == ids, 1.0, 0.0).astype(BF16)


def kernel(
    patches,
    feat_ref, sender_ref, receiver_ref, offset_ref, link_sender_ref, link_receiver_ref, fw_ref,
    grid_hbm, mesh_hbm, link_hbm, *rest,
):
    weights_hbm = rest[:WEIGHTS]
    out_ref = rest[WEIGHTS]
    (
        grid, mesh, link, weights,
        tab1, tab2, src, emb, pre, link_pre, fresh,
        sib_out, sib_in, z_out, z_in, y_out, y_in, y_own, m_own, mesh_next, link_dst,
        in_sems, ex_send, ex_recv, sib_send, sib_recv, z_send, z_recv, y_send, y_recv,
    ) = rest[WEIGHTS + 1 :]
    rows = mesh.shape[0]
    edges = fresh.shape[0]
    span = 2 * REACH + 1
    part = rows // CHUNKS
    chip = lax.axis_index("patch")
    core = lax.axis_index("band")
    odd = lax.rem(chip, 2)
    partner = chip + 1 - 2 * odd
    up = lax.rem(chip + 2, patches)
    down = lax.rem(chip + patches - 2, patches)
    cast_to = up * (1 - odd) + down * odd
    fold_to = down * (1 - odd) + up * odd
    to_sib = {"patch": chip, "band": 1 - core}
    to_partner = {"patch": partner, "band": core}
    to_cast = {"patch": cast_to, "band": core}
    to_fold = {"patch": fold_to, "band": core}

    barrier = pltpu.get_barrier_semaphore()
    for where in (to_sib, to_partner, to_cast, to_fold):
        pl.semaphore_signal(barrier, inc=1, device_id=where, device_id_type=pl.DeviceIdType.MESH)

    loads = [
        pltpu.make_async_copy(weights_hbm[at], weights.at[at], in_sems.at[at])
        for at in range(WEIGHTS)
    ]
    (w_target, w_source, w_edge, w_edge2, w_first, w_summed, w_second,
     w_link, w_lsrc, w_ldst, w_link2, w_vfirst, w_vsummed, w_vsecond) = range(WEIGHTS)
    load_grid = pltpu.make_async_copy(grid_hbm, grid, in_sems.at[WEIGHTS])
    load_mesh = pltpu.make_async_copy(mesh_hbm, mesh, in_sems.at[WEIGHTS + 1])
    load_link = pltpu.make_async_copy(link_hbm, link, in_sems.at[WEIGHTS + 2])
    load_mesh.start()
    loads[w_target].start()
    load_grid.start()
    for at in (w_source, w_edge, w_edge2):
        loads[at].start()
    load_link.start()
    for at in range(w_first, WEIGHTS):
        loads[at].start()

    def remote(source, target, send, recv, where):
        return pltpu.make_async_remote_copy(
            src_ref=source, dst_ref=target, send_sem=send, recv_sem=recv,
            device_id=where, device_id_type=pl.DeviceIdType.MESH,
        )

    class Multicast:
        def __init__(self, tab, which):
            def slot(index, at):
                return tab.at[pl.ds(pl.multiple_of(index * rows + at * part, part), part)]

            def sems(at):
                return ex_send.at[which, at], ex_recv.at[which, at]

            own = 2 + core
            there = 4 * odd + core
            from_partner = 4 * (1 - odd) + core
            from_far = 4 * odd + core
            self.own, self.y, self.z, self.ysib, self.zsib = [], [], [], [], []
            for at in range(CHUNKS):
                base = 5 * at
                self.own.append(remote(slot(own, at), slot(own, at), *sems(base), to_sib))
                self.y.append(remote(slot(own, at), slot(there, at), *sems(base + 1), to_partner))
                self.z.append(remote(slot(from_partner, at), slot(there, at), *sems(base + 2), to_cast))
                self.ysib.append(remote(slot(from_partner, at), slot(from_partner, at), *sems(base + 3), to_sib))
                self.zsib.append(remote(slot(from_far, at), slot(from_far, at), *sems(base + 4), to_sib))

        def start(self):
            for at in range(CHUNKS):
                self.y[at].start()
            for at in range(CHUNKS):
                self.own[at].start()

        def relay(self):
            for at in range(CHUNKS):
                self.y[at].wait_recv()
                self.z[at].start()
                self.ysib[at].start()

        def finish(self):
            for at in range(CHUNKS):
                self.z[at].wait_recv()
                self.zsib[at].start()
            for at in range(CHUNKS):
                self.own[at].wait_recv()
                self.ysib[at].wait_recv()
                self.zsib[at].wait_recv()

        def drain(self):
            for at in range(CHUNKS):
                for copy in (self.own[at], self.y[at], self.z[at], self.ysib[at], self.zsib[at]):
                    copy.wait_send()

    def tiles(count, step):
        def go(at, carry):
            step(pl.ds(pl.multiple_of(at * TILE, TILE), TILE))
            return carry

        lax.fori_loop(0, count // TILE, go, 0)

    own_rows = pl.ds(pl.multiple_of((2 + core) * rows, rows), rows)
    near = pl.ds(pl.multiple_of(core * rows, rows), span * rows)
    load_mesh.wait()
    loads[w_target].wait()
    tab1[own_rows, :] = mm(mesh[...], weights[w_target]).astype(BF16)
    pl.semaphore_wait(barrier, 4)
    cast1 = Multicast(tab1, 0)
    cast1.start()

    keys = []
    for at in range(edges // BLOCK):
        keys.append(
            receiver_ref[:, at * BLOCK : (at + 1) * BLOCK] + (offset_ref[at] + REACH) * rows
        )
    edge_key = jnp.concatenate(keys, axis=1)

    load_grid.wait()
    loads[w_source].wait()

    def project_source(at):
        src[at, :] = mm(grid[at, :], weights[w_source]).astype(BF16)

    tiles(src.shape[0], project_source)
    emb[...] = lax.dot_general(
        feat_ref[...], fw_ref[...], (((0,), (0,)), ((), ())), preferred_element_type=F32
    ).astype(BF16)
    cast1.relay()
    loads[w_edge].wait()
    for at in range(edges // TILE):
        here = pl.ds(at * TILE, TILE)
        hot = one_hot_rows(sender_ref[:, at * TILE : (at + 1) * TILE], src.shape[0])
        pre[here, :] = mm(emb[here, :], weights[w_edge]) + mm(hot, src[...])
    loads[w_edge2].wait()
    cast1.finish()

    for at in range(edges // TILE):
        here = pl.ds(at * TILE, TILE)
        hot = one_hot_rows(edge_key[:, at * TILE : (at + 1) * TILE], span * rows)
        hidden = silu(pre[here, :] + mm(hot, tab1[near, :])).astype(BF16)
        fresh[here, :] = (
            emb[here, :].astype(F32) + normalize(mm(hidden, weights[w_edge2]))
        ).astype(BF16)
    cast1.drain()

    jz = 2 * odd
    jy = 2 * (1 - odd)
    slot_key = edge_key + core * rows

    def partial(slot):
        return mm(one_hot_columns(slot_key, slot * rows, rows), fresh[...])

    order = (jz, jy, 1)
    sibs = []
    for at in range(3):
        sib_out[at] = partial(2 * order[at] + 1 - core).astype(BF16)
        copy = remote(sib_out.at[at], sib_in.at[at], sib_send.at[at], sib_recv.at[at], to_sib)
        copy.start()
        sibs.append(copy)
        if at == 0:
            far = partial(2 * jz + core)
            copy.wait_recv()
            z_out[...] = (far + sib_in[0].astype(F32)).astype(BF16)
            z_copies = []
            for chunk in range(CHUNKS):
                piece = pl.ds(chunk * part, part)
                z_copies.append(
                    remote(z_out.at[piece], z_in.at[piece], z_send.at[chunk], z_recv.at[chunk], to_fold)
                )
                z_copies[-1].start()
    y_own[...] = partial(2 * jy + core)
    m_own[...] = partial(2 + core)
    sibs[1].wait_recv()
    y_own[...] += sib_in[1].astype(F32)
    sibs[2].wait_recv()
    m_own[...] += sib_in[2].astype(F32)
    y_copies = []
    for chunk in range(CHUNKS):
        piece = pl.ds(chunk * part, part)
        z_copies[chunk].wait_recv()
        y_out[piece, :] = (y_own[piece, :] + z_in[piece, :].astype(F32)).astype(BF16)
        y_copies.append(
            remote(y_out.at[piece], y_in.at[piece], y_send.at[chunk], y_recv.at[chunk], to_partner)
        )
        y_copies[-1].start()
    load_link.wait()
    loads[w_link].wait()

    def project_link(at):
        link_pre[at, :] = mm(link[at, :], weights[w_link])

    tiles(edges, project_link)
    for at in (w_first, w_summed, w_second, w_lsrc, w_ldst, w_link2, w_vfirst, w_vsummed, w_vsecond):
        loads[at].wait()
    node_pre = mm(mesh[...], weights[w_first])
    for chunk in range(CHUNKS):
        y_copies[chunk].wait_recv()
    summed = (m_own[...] + y_in[...].astype(F32)).astype(BF16)
    hidden = silu(node_pre + mm(summed, weights[w_summed])).astype(BF16)
    mesh_next[...] = (
        mesh[...].astype(F32) + normalize(mm(hidden, weights[w_second]))
    ).astype(BF16)
    for copy in sibs + z_copies + y_copies:
        copy.wait_send()

    tab2[own_rows, :] = mm(mesh_next[...], weights[w_lsrc]).astype(BF16)
    cast2 = Multicast(tab2, 1)
    cast2.start()
    link_dst[...] = mm(mesh_next[...], weights[w_ldst]).astype(BF16)
    for at in range(edges // TILE):
        here = pl.ds(at * TILE, TILE)
        hot = one_hot_rows(link_receiver_ref[:, at * TILE : (at + 1) * TILE], rows)
        link_pre[here, :] += mm(hot, link_dst[...])
        if at == 1:
            cast2.relay()
    y_own[...] = mm(mesh_next[...], weights[w_vfirst])
    total = 2 * patches
    bits = rows.bit_length() - 1
    sender = link_sender_ref[...]
    place = lax.shift_right_logical(sender, bits) - (2 * chip + core) + REACH
    place = jnp.where(place < 0, place + total, place)
    place = jnp.where(place >= total, place - total, place)
    link_key = place * rows + lax.bitwise_and(sender, rows - 1)
    cast2.finish()

    for at in range(edges // TILE):
        here = pl.ds(at * TILE, TILE)
        hot = one_hot_rows(link_key[:, at * TILE : (at + 1) * TILE], span * rows)
        hidden = silu(link_pre[here, :] + mm(hot, tab2[near, :])).astype(BF16)
        fresh[here, :] = (
            link[here, :].astype(F32) + normalize(mm(hidden, weights[w_link2]))
        ).astype(BF16)
    link_sum = mm(one_hot_columns(link_receiver_ref[...], 0, rows), fresh[...]).astype(BF16)
    hidden = silu(y_own[...] + mm(link_sum, weights[w_vsummed])).astype(BF16)
    out_ref[...] = (
        mesh_next[...].astype(F32) + normalize(mm(hidden, weights[w_vsecond]))
    ).astype(BF16)
    cast2.drain()


def body(
    patches,
    grid_latent, mesh_latent, edge_features, edge_sender, edge_receiver, block_offset,
    link_latent, link_sender, link_receiver, feature_weight, source_weight, target_weight,
    edge_weight, edge_second, node_first, node_summed, node_second, link_weight, link_source,
    link_target, link_second, vertex_first, vertex_summed, vertex_second,
):
    rows, width = mesh_latent.shape
    edges = edge_sender.shape[0]
    vmem = pl.BlockSpec(memory_space=pltpu.VMEM)
    smem = pl.BlockSpec(memory_space=pltpu.SMEM)
    anywhere = pl.BlockSpec(memory_space=pl.ANY)
    dma = pltpu.SemaphoreType.DMA
    table = pltpu.VMEM((6 * rows, width), BF16)
    flat = pltpu.VMEM((rows, width), BF16)
    return pl.pallas_call(
        functools.partial(kernel, patches),
        out_shape=jax.ShapeDtypeStruct((rows, width), BF16),
        in_specs=[vmem, vmem, vmem, smem, vmem, vmem, vmem] + [anywhere] * (3 + WEIGHTS),
        out_specs=vmem,
        scratch_shapes=[
            pltpu.VMEM(grid_latent.shape, BF16),
            flat,
            pltpu.VMEM(link_latent.shape, BF16),
            pltpu.VMEM((WEIGHTS, width, width), BF16),
            table,
            table,
            pltpu.VMEM((grid_latent.shape[0], width), BF16),
            pltpu.VMEM((edges, width), BF16),
            pltpu.VMEM((edges, width), F32),
            pltpu.VMEM((edges, width), F32),
            pltpu.VMEM((edges, width), BF16),
            pltpu.VMEM((3, rows, width), BF16),
            pltpu.VMEM((3, rows, width), BF16),
            flat, flat, flat, flat,
            pltpu.VMEM((rows, width), F32),
            pltpu.VMEM((rows, width), F32),
            flat, flat,
            dma((WEIGHTS + 3,)),
            dma((2, 5 * CHUNKS)), dma((2, 5 * CHUNKS)),
            dma((3,)), dma((3,)),
            dma((CHUNKS,)), dma((CHUNKS,)),
            dma((CHUNKS,)), dma((CHUNKS,)),
        ],
        compiler_params=pltpu.CompilerParams(
            collective_id=0, has_side_effects=True, vmem_limit_bytes=48 * 1024 * 1024
        ),
    )(
        edge_features, edge_sender.reshape(1, -1), edge_receiver.reshape(1, -1), block_offset,
        link_sender.reshape(1, -1), link_receiver.reshape(1, -1), feature_weight,
        grid_latent, mesh_latent, link_latent,
        target_weight, source_weight, edge_weight, edge_second, node_first, node_summed,
        node_second, link_weight, link_source, link_target, link_second, vertex_first,
        vertex_summed, vertex_second,
    )


def solution(mesh):
    rows = P(AXES, None)
    flat = P(AXES)
    placed = (rows, rows, P(None, AXES), flat, flat, flat, rows, flat, flat) + (P(),) * 15
    return jax.shard_map(
        functools.partial(body, mesh.shape["patch"]),
        mesh=mesh,
        in_specs=placed,
        out_specs=rows,
        check_vma=False,
    )
```

time: 149 us -> 70.6 us (0.47)
  the two profiles are of different devices: /device:TPU:0 before, /device:TPU:1 now
where the time goes in v1:
time: 70.6 us; the launch traced here: 69.8 us
  Pallas kernels  53.6 us (76%)
  local copies, waits for them, and re-layouts  16.2 us (23%)
    pallas_call x1, Pallas kernels, body(): pl.pallas_call(functools.partial(kernel, patches), out_shape=jax.ShapeDty...  53.6 us
    unnamed x37, local copies, waits for them, and re-layouts  16.2 us

profile of v1, /device:TPU:1, one launch (start us, length us, event | category | flops | bytes accessed | tf_op | source)
XLA Modules:
  0.0 69.8 jit_solution(9778715663009737023)
XLA Ops:
  0.0 0.0 copy-start.12
  0.0 0.0 copy-start.17
  0.0 0.7 copy-done.12
  0.7 0.0 copy-done.17
  0.7 0.0 copy-start
  0.7 1.0 %copy-done = bf16[512,512]{1,0:T(8,128)(2,1)S(1)} copy-done((bf16[512,512]{1,0:T(8,128)(2,1)S(1)}, bf16[512,512]{1,0:T(8,128)(2,1)}, u32[]{:S(2)}) %copy-start) | copy-done | bytes 524312
  1.7 0.0 copy-start.1
  1.7 1.0 %copy-done.1 = bf16[512,512]{1,0:T(8,128)(2,1)S(1)} copy-done((bf16[512,512]{1,0:T(8,128)(2,1)S(1)}, bf16[512,512]{1,0:T(8,128)(2,1)}, u32[]{:S(2)}) %copy-start.1) | copy-done | bytes 524312
  2.8 0.0 copy-start.2
  2.8 1.0 %copy-done.2 = bf16[512,512]{1,0:T(8,128)(2,1)S(1)} copy-done((bf16[512,512]{1,0:T(8,128)(2,1)S(1)}, bf16[512,512]{1,0:T(8,128)(2,1)}, u32[]{:S(2)}) %copy-start.2) | copy-done | bytes 524312
  3.8 0.0 copy-start.3
  3.8 1.0 %copy-done.3 = bf16[512,512]{1,0:T(8,128)(2,1)S(1)} copy-done((bf16[512,512]{1,0:T(8,128)(2,1)S(1)}, bf16[512,512]{1,0:T(8,128)(2,1)}, u32[]{:S(2)}) %copy-start.3) | copy-done | bytes 524312
  4.9 0.0 copy-start.4
  4.9 1.0 %copy-done.4 = bf16[512,512]{1,0:T(8,128)(2,1)S(1)} copy-done((bf16[512,512]{1,0:T(8,128)(2,1)S(1)}, bf16[512,512]{1,0:T(8,128)(2,1)}, u32[]{:S(2)}) %copy-start.4) | copy-done | bytes 524312
  5.9 0.0 copy-start.5
  5.9 1.0 %copy-done.5 = bf16[512,512]{1,0:T(8,128)(2,1)S(1)} copy-done((bf16[512,512]{1,0:T(8,128)(2,1)S(1)}, bf16[512,512]{1,0:T(8,128)(2,1)}, u32[]{:S(2)}) %copy-start.5) | copy-done | bytes 524312
  6.9 0.0 copy-start.6
  6.9 1.0 %copy-done.6 = bf16[512,512]{1,0:T(8,128)(2,1)S(1)} copy-done((bf16[512,512]{1,0:T(8,128)(2,1)S(1)}, bf16[512,512]{1,0:T(8,128)(2,1)}, u32[]{:S(2)}) %copy-start.6) | copy-done | bytes 524312
  8.0 0.0 copy-start.7
  8.0 1.0 %copy-done.7 = bf16[512,512]{1,0:T(8,128)(2,1)S(1)} copy-done((bf16[512,512]{1,0:T(8,128)(2,1)S(1)}, bf16[512,512]{1,0:T(8,128)(2,1)}, u32[]{:S(2)}) %copy-start.7) | copy-done | bytes 524312
  9.0 0.0 copy-start.8
  9.0 1.0 %copy-done.8 = bf16[512,512]{1,0:T(8,128)(2,1)S(1)} copy-done((bf16[512,512]{1,0:T(8,128)(2,1)S(1)}, bf16[512,512]{1,0:T(8,128)(2,1)}, u32[]{:S(2)}) %copy-start.8) | copy-done | bytes 524312
  10.1 0.0 copy-start.9
  10.1 1.0 %copy-done.9 = bf16[512,512]{1,0:T(8,128)(2,1)S(1)} copy-done((bf16[512,512]{1,0:T(8,128)(2,1)S(1)}, bf16[512,512]{1,0:T(8,128)(2,1)}, u32[]{:S(2)}) %copy-start.9) | copy-done | bytes 524312
  11.1 0.0 copy-start.10
  11.1 0.9 %copy-done.10 = bf16[256,512]{1,0:T(8,128)(2,1)S(1)} copy-done((bf16[256,512]{1,0:T(8,128)(2,1)S(1)}, bf16[256,512]{1,0:T(8,128)(2,1)}, u32[]{:S(2)}) %copy-start.10) | copy-done | bytes 262168
  12.1 0.0 copy-start.11
  12.1 0.7 copy-done.11
  12.8 0.0 copy-start.13
  12.8 0.7 copy-done.13
  13.4 0.0 copy-start.14
  13.4 0.7 copy-done.14
  14.1 0.0 copy-start.15
  14.1 0.7 copy-done.15
  14.8 0.0 copy-start.16
  14.8 0.7 copy-done.16
  15.5 53.6 %shard_map.226 = bf16[256,512]{1,0:T(8,128)(2,1)S(1)} custom-call(bf16[4,1024]{1,0:T(4,128)(2,1)S(1)} %copy-done.11, s32[1,1024]{1,0:T(1,128)S(1)} %bitcast.4, s32[1,1024]{1,0:T(1,128)S(1)} %bitcast.5, s32[8]{0:T(128)S(1)} %copy-done.17, s32[1,1024]{1,0:T(1,128)S(1)} %bitcast.6, s32[1,1024]{1,0:T(1,128)S(1)} %bitcast.7, bf16[4,512]{1,0:T(4,128)(2,1)S(1)} %copy-done.16, ...), custom_call_target="tpu_custom_call" | custom-call | tf_op jit(solution)/shard_map/pallas_call | solution.py:324
  69.1 0.7 %copy.26 = bf16[256,512]{1,0:T(8,128)(2,1)} copy(bf16[256,512]{1,0:T(8,128)(2,1)S(1)} %shard_map.226) | data formatting | bytes 524288
Async XLA Ops:
  0.0 0.7 copy-start.12
  0.0 0.7 copy-start.17
  0.7 1.0 %copy-start = (bf16[512,512]{1,0:T(8,128)(2,1)S(1)}, bf16[512,512]{1,0:T(8,128)(2,1)}, u32[]{:S(2)}) copy-start(bf16[512,512]{1,0:T(8,128)(2,1)} %rest_0_.1) | copy-start | bytes 1572868
  1.7 1.0 %copy-start.1 = (bf16[512,512]{1,0:T(8,128)(2,1)S(1)}, bf16[512,512]{1,0:T(8,128)(2,1)}, u32[]{:S(2)}) copy-start(bf16[512,512]{1,0:T(8,128)(2,1)} %rest_1_.1) | copy-start | bytes 1572868
  2.8 1.0 %copy-start.2 = (bf16[512,512]{1,0:T(8,128)(2,1)S(1)}, bf16[512,512]{1,0:T(8,128)(2,1)}, u32[]{:S(2)}) copy-start(bf16[512,512]{1,0:T(8,128)(2,1)} %rest_2_.1) | copy-start | bytes 1572868
  3.8 1.0 %copy-start.3 = (bf16[512,512]{1,0:T(8,128)(2,1)S(1)}, bf16[512,512]{1,0:T(8,128)(2,1)}, u32[]{:S(2)}) copy-start(bf16[512,512]{1,0:T(8,128)(2,1)} %rest_3_.1) | copy-start | bytes 1572868
  4.9 1.0 %copy-start.4 = (bf16[512,512]{1,0:T(8,128)(2,1)S(1)}, bf16[512,512]{1,0:T(8,128)(2,1)}, u32[]{:S(2)}) copy-start(bf16[512,512]{1,0:T(8,128)(2,1)} %rest_4_.1) | copy-start | bytes 1572868
  5.9 1.0 %copy-start.5 = (bf16[512,512]{1,0:T(8,128)(2,1)S(1)}, bf16[512,512]{1,0:T(8,128)(2,1)}, u32[]{:S(2)}) copy-start(bf16[512,512]{1,0:T(8,128)(2,1)} %rest_5_.1) | copy-start | bytes 1572868
  6.9 1.0 %copy-start.6 = (bf16[512,512]{1,0:T(8,128)(2,1)S(1)}, bf16[512,512]{1,0:T(8,128)(2,1)}, u32[]{:S(2)}) copy-start(bf16[512,512]{1,0:T(8,128)(2,1)} %rest_6_.1) | copy-start | bytes 1572868
  8.0 1.0 %copy-start.7 = (bf16[512,512]{1,0:T(8,128)(2,1)S(1)}, bf16[512,512]{1,0:T(8,128)(2,1)}, u32[]{:S(2)}) copy-start(bf16[512,512]{1,0:T(8,128)(2,1)} %rest_7_.1) | copy-start | bytes 1572868
  9.0 1.0 %copy-start.8 = (bf16[512,512]{1,0:T(8,128)(2,1)S(1)}, bf16[512,512]{1,0:T(8,128)(2,1)}, u32[]{:S(2)}) copy-start(bf16[512,512]{1,0:T(8,128)(2,1)} %rest_8_.1) | copy-start | bytes 1572868
  10.1 1.0 %copy-start.9 = (bf16[512,512]{1,0:T(8,128)(2,1)S(1)}, bf16[512,512]{1,0:T(8,128)(2,1)}, u32[]{:S(2)}) copy-start(bf16[512,512]{1,0:T(8,128)(2,1)} %rest_9_.1) | copy-start | bytes 1572868
  11.1 0.9 %copy-start.10 = (bf16[256,512]{1,0:T(8,128)(2,1)S(1)}, bf16[256,512]{1,0:T(8,128)(2,1)}, u32[]{:S(2)}) copy-start(bf16[256,512]{1,0:T(8,128)(2,1)} %mesh_hbm.1) | copy-start | bytes 786436
  12.1 0.7 copy-start.11
  12.8 0.7 copy-start.13
  13.4 0.7 copy-start.14
  14.1 0.7 copy-start.15
  14.8 0.7 copy-start.16

commit v2 on v1

--- a/solution.py
+++ b/solution.py
@@ -10,8 +10,8 @@
 REACH = 2
 BLOCK = 128
 EPSILON = 1e-05
-CHUNKS = 2
-TILE = 256
+CHUNKS = 4
+TILE = 512
 LANES = 128
 AXES = ("replica", "patch", "band")
 BF16 = jnp.bfloat16
@@ -65,12 +65,11 @@
     (
         grid, mesh, link, weights,
         tab1, tab2, src, emb, pre, link_pre, fresh,
-        sib_out, sib_in, z_out, z_in, y_out, y_in, y_own, m_own, mesh_next, link_dst,
+        sib_out, sib_in, z_out, z_in, y_out, y_in, z_own, y_own, m_own, mesh_next, link_dst,
         in_sems, ex_send, ex_recv, sib_send, sib_recv, z_send, z_recv, y_send, y_recv,
     ) = rest[WEIGHTS + 1 :]
     rows = mesh.shape[0]
     edges = fresh.shape[0]
-    span = 2 * REACH + 1
     part = rows // CHUNKS
     chip = lax.axis_index("patch")
     core = lax.axis_index("band")
@@ -100,12 +99,6 @@
     load_link = pltpu.make_async_copy(link_hbm, link, in_sems.at[WEIGHTS + 2])
     load_mesh.start()
     loads[w_target].start()
-    load_grid.start()
-    for at in (w_source, w_edge, w_edge2):
-        loads[at].start()
-    load_link.start()
-    for at in range(w_first, WEIGHTS):
-        loads[at].start()
 
     def remote(source, target, send, recv, where):
         return pltpu.make_async_remote_copy(
@@ -134,25 +127,26 @@
                 self.ysib.append(remote(slot(from_partner, at), slot(from_partner, at), *sems(base + 3), to_sib))
                 self.zsib.append(remote(slot(from_far, at), slot(from_far, at), *sems(base + 4), to_sib))
 
-        def start(self):
-            for at in range(CHUNKS):
-                self.y[at].start()
-            for at in range(CHUNKS):
-                self.own[at].start()
-
-        def relay(self):
-            for at in range(CHUNKS):
-                self.y[at].wait_recv()
-                self.z[at].start()
-                self.ysib[at].start()
-
-        def finish(self):
-            for at in range(CHUNKS):
-                self.z[at].wait_recv()
-                self.zsib[at].start()
+        def start(self, at):
+            self.y[at].start()
+            self.own[at].start()
+
+        def relay(self, at):
+            self.y[at].wait_recv()
+            self.z[at].start()
+            self.ysib[at].start()
+
+        def nearby(self):
             for at in range(CHUNKS):
                 self.own[at].wait_recv()
                 self.ysib[at].wait_recv()
+
+        def pass_far(self, at):
+            self.z[at].wait_recv()
+            self.zsib[at].start()
+
+        def finish(self):
+            for at in range(CHUNKS):
                 self.zsib[at].wait_recv()
 
         def drain(self):
@@ -168,23 +162,52 @@
         lax.fori_loop(0, count // TILE, go, 0)
 
     own_rows = pl.ds(pl.multiple_of((2 + core) * rows, rows), rows)
-    near = pl.ds(pl.multiple_of(core * rows, rows), span * rows)
+    near_first = 2 * (1 - odd) * rows
+    far_first = 4 * odd * rows
+    near = pl.ds(pl.multiple_of(near_first, rows), 4 * rows)
+    far_rows = pl.ds(pl.multiple_of(far_first, rows), 2 * rows)
+
+    def gather_near(cast, tab, keys, total):
+        cast.nearby()
+        passed = 0
+        for at in range(edges // TILE):
+            here = pl.ds(at * TILE, TILE)
+            hot = one_hot_rows(keys[:, at * TILE : (at + 1) * TILE] - near_first, 4 * rows)
+            total[here, :] += mm(hot, tab[near, :])
+            if passed < CHUNKS:
+                cast.pass_far(passed)
+                passed += 1
+        for at in range(passed, CHUNKS):
+            cast.pass_far(at)
+        cast.finish()
+
+    def gather_far(tab, keys, at):
+        hot = one_hot_rows(keys[:, at * TILE : (at + 1) * TILE] - far_first, 2 * rows)
+        return mm(hot, tab[far_rows, :])
+
     load_mesh.wait()
     loads[w_target].wait()
+    load_grid.start()
+    for at in (w_source, w_edge, w_edge2):
+        loads[at].start()
     tab1[own_rows, :] = mm(mesh[...], weights[w_target]).astype(BF16)
     pl.semaphore_wait(barrier, 4)
     cast1 = Multicast(tab1, 0)
-    cast1.start()
+    for chunk in range(CHUNKS):
+        cast1.start(chunk)
 
     keys = []
     for at in range(edges // BLOCK):
         keys.append(
             receiver_ref[:, at * BLOCK : (at + 1) * BLOCK] + (offset_ref[at] + REACH) * rows
         )
-    edge_key = jnp.concatenate(keys, axis=1)
+    slot_key = jnp.concatenate(keys, axis=1) + core * rows
 
     load_grid.wait()
     loads[w_source].wait()
+    load_link.start()
+    for at in range(w_first, WEIGHTS):
+        loads[at].start()
 
     def project_source(at):
         src[at, :] = mm(grid[at, :], weights[w_source]).astype(BF16)
@@ -193,19 +216,23 @@
     emb[...] = lax.dot_general(
         feat_ref[...], fw_ref[...], (((0,), (0,)), ((), ())), preferred_element_type=F32
     ).astype(BF16)
-    cast1.relay()
     loads[w_edge].wait()
+    passed = 0
     for at in range(edges // TILE):
+        if passed < CHUNKS:
+            cast1.relay(passed)
+            passed += 1
         here = pl.ds(at * TILE, TILE)
         hot = one_hot_rows(sender_ref[:, at * TILE : (at + 1) * TILE], src.shape[0])
         pre[here, :] = mm(emb[here, :], weights[w_edge]) + mm(hot, src[...])
+    for at in range(passed, CHUNKS):
+        cast1.relay(at)
     loads[w_edge2].wait()
-    cast1.finish()
+    gather_near(cast1, tab1, slot_key, pre)
 
     for at in range(edges // TILE):
         here = pl.ds(at * TILE, TILE)
-        hot = one_hot_rows(edge_key[:, at * TILE : (at + 1) * TILE], span * rows)
-        hidden = silu(pre[here, :] + mm(hot, tab1[near, :])).astype(BF16)
+        hidden = silu(pre[here, :] + gather_far(tab1, slot_key, at)).astype(BF16)
         fresh[here, :] = (
             emb[here, :].astype(F32) + normalize(mm(hidden, weights[w_edge2]))
         ).astype(BF16)
@@ -213,74 +240,99 @@
 
     jz = 2 * odd
     jy = 2 * (1 - odd)
-    slot_key = edge_key + core * rows
 
     def partial(slot):
         return mm(one_hot_columns(slot_key, slot * rows, rows), fresh[...])
 
-    order = (jz, jy, 1)
+    pieces = [pl.ds(chunk * part, part) for chunk in range(CHUNKS)]
+    sib_out[0] = partial(2 * jz + 1 - core).astype(BF16)
     sibs = []
-    for at in range(3):
-        sib_out[at] = partial(2 * order[at] + 1 - core).astype(BF16)
-        copy = remote(sib_out.at[at], sib_in.at[at], sib_send.at[at], sib_recv.at[at], to_sib)
-        copy.start()
-        sibs.append(copy)
-        if at == 0:
-            far = partial(2 * jz + core)
-            copy.wait_recv()
-            z_out[...] = (far + sib_in[0].astype(F32)).astype(BF16)
-            z_copies = []
-            for chunk in range(CHUNKS):
-                piece = pl.ds(chunk * part, part)
-                z_copies.append(
-                    remote(z_out.at[piece], z_in.at[piece], z_send.at[chunk], z_recv.at[chunk], to_fold)
-                )
-                z_copies[-1].start()
+    for chunk in range(CHUNKS):
+        sibs.append(
+            remote(
+                sib_out.at[0, pieces[chunk]], sib_in.at[0, pieces[chunk]],
+                sib_send.at[chunk], sib_recv.at[chunk], to_sib,
+            )
+        )
+        sibs[-1].start()
+    z_own[...] = partial(2 * jz + core)
+    sib_out[1] = partial(2 * jy + 1 - core).astype(BF16)
+    z_copies = []
+    y_copies = []
+    for chunk in range(CHUNKS):
+        piece = pieces[chunk]
+        sibs[chunk].wait_recv()
+        z_out[piece, :] = (z_own[piece, :] + sib_in[0, piece, :].astype(F32)).astype(BF16)
+        z_copies.append(
+            remote(z_out.at[piece], z_in.at[piece], z_send.at[chunk], z_recv.at[chunk], to_fold)
+        )
+        z_copies[-1].start()
+        y_copies.append(
+            remote(y_out.at[piece], y_in.at[piece], y_send.at[chunk], y_recv.at[chunk], to_partner)
+        )
+    for at in (1, 2):
+        if at == 2:
+            sib_out[2] = partial(3 - core).astype(BF16)
+        sibs.append(
+            remote(
+                sib_out.at[at], sib_in.at[at],
+                sib_send.at[CHUNKS + at - 1], sib_recv.at[CHUNKS + at - 1], to_sib,
+            )
+        )
+        sibs[-1].start()
     y_own[...] = partial(2 * jy + core)
     m_own[...] = partial(2 + core)
-    sibs[1].wait_recv()
+    sibs[CHUNKS].wait_recv()
     y_own[...] += sib_in[1].astype(F32)
-    sibs[2].wait_recv()
-    m_own[...] += sib_in[2].astype(F32)
-    y_copies = []
-    for chunk in range(CHUNKS):
-        piece = pl.ds(chunk * part, part)
+    for at in (w_first, w_summed, w_second, w_link, w_lsrc, w_ldst, w_link2, w_vfirst, w_vsummed, w_vsecond):
+        loads[at].wait()
+    load_link.wait()
+    cast2 = Multicast(tab2, 1)
+
+    def forward(chunk):
+        piece = pieces[chunk]
         z_copies[chunk].wait_recv()
         y_out[piece, :] = (y_own[piece, :] + z_in[piece, :].astype(F32)).astype(BF16)
-        y_copies.append(
-            remote(y_out.at[piece], y_in.at[piece], y_send.at[chunk], y_recv.at[chunk], to_partner)
-        )
-        y_copies[-1].start()
-    load_link.wait()
-    loads[w_link].wait()
+        y_copies[chunk].start()
+
+    def node(chunk):
+        piece = pieces[chunk]
+        y_copies[chunk].wait_recv()
+        summed = (m_own[piece, :] + y_in[piece, :].astype(F32)).astype(BF16)
+        hidden = silu(z_own[piece, :] + mm(summed, weights[w_summed])).astype(BF16)
+        new = (
+            mesh[piece, :].astype(F32) + normalize(mm(hidden, weights[w_second]))
+        ).astype(BF16)
+        mesh_next[piece, :] = new
+        sends = pl.ds(pl.multiple_of((2 + core) * rows + chunk * part, part), part)
+        tab2[sends, :] = mm(new, weights[w_lsrc]).astype(BF16)
+        cast2.start(chunk)
 
     def project_link(at):
         link_pre[at, :] = mm(link[at, :], weights[w_link])
 
+    forward(0)
+    z_own[...] = mm(mesh[...], weights[w_first])
+    sibs[CHUNKS + 1].wait_recv()
+    m_own[...] += sib_in[2].astype(F32)
+    for chunk in range(1, CHUNKS):
+        forward(chunk)
+        node(chunk - 1)
+        if chunk > 2:
+            cast2.relay(chunk - 3)
+    node(CHUNKS - 1)
     tiles(edges, project_link)
-    for at in (w_first, w_summed, w_second, w_lsrc, w_ldst, w_link2, w_vfirst, w_vsummed, w_vsecond):
-        loads[at].wait()
-    node_pre = mm(mesh[...], weights[w_first])
-    for chunk in range(CHUNKS):
-        y_copies[chunk].wait_recv()
-    summed = (m_own[...] + y_in[...].astype(F32)).astype(BF16)
-    hidden = silu(node_pre + mm(summed, weights[w_summed])).astype(BF16)
-    mesh_next[...] = (
-        mesh[...].astype(F32) + normalize(mm(hidden, weights[w_second]))
-    ).astype(BF16)
-    for copy in sibs + z_copies + y_copies:
-        copy.wait_send()
-
-    tab2[own_rows, :] = mm(mesh_next[...], weights[w_lsrc]).astype(BF16)
-    cast2 = Multicast(tab2, 1)
-    cast2.start()
+    passed = max(CHUNKS - 3, 0)
     link_dst[...] = mm(mesh_next[...], weights[w_ldst]).astype(BF16)
     for at in range(edges // TILE):
+        if passed < CHUNKS:
+            cast2.relay(passed)
+            passed += 1
         here = pl.ds(at * TILE, TILE)
         hot = one_hot_rows(link_receiver_ref[:, at * TILE : (at + 1) * TILE], rows)
         link_pre[here, :] += mm(hot, link_dst[...])
-        if at == 1:
-            cast2.relay()
+    for at in range(passed, CHUNKS):
+        cast2.relay(at)
     y_own[...] = mm(mesh_next[...], weights[w_vfirst])
     total = 2 * patches
     bits = rows.bit_length() - 1
@@ -288,13 +340,12 @@
     place = lax.shift_right_logical(sender, bits) - (2 * chip + core) + REACH
     place = jnp.where(place < 0, place + total, place)
     place = jnp.where(place >= total, place - total, place)
-    link_key = place * rows + lax.bitwise_and(sender, rows - 1)
-    cast2.finish()
+    link_key = (place + core) * rows + lax.bitwise_and(sender, rows - 1)
+    gather_near(cast2, tab2, link_key, link_pre)
 
     for at in range(edges // TILE):
         here = pl.ds(at * TILE, TILE)
-        hot = one_hot_rows(link_key[:, at * TILE : (at + 1) * TILE], span * rows)
-        hidden = silu(link_pre[here, :] + mm(hot, tab2[near, :])).astype(BF16)
+        hidden = silu(link_pre[here, :] + gather_far(tab2, link_key, at)).astype(BF16)
         fresh[here, :] = (
             link[here, :].astype(F32) + normalize(mm(hidden, weights[w_link2]))
         ).astype(BF16)
@@ -304,6 +355,8 @@
         mesh_next[...].astype(F32) + normalize(mm(hidden, weights[w_vsecond]))
     ).astype(BF16)
     cast2.drain()
+    for copy in sibs + z_copies + y_copies:
+        copy.wait_send()
 
 
 def body(
@@ -317,7 +370,7 @@
     edges = edge_sender.shape[0]
     vmem = pl.BlockSpec(memory_space=pltpu.VMEM)
     smem = pl.BlockSpec(memory_space=pltpu.SMEM)
-    anywhere = pl.BlockSpec(memory_space=pl.ANY)
+    anywhere = pl.BlockSpec(memory_space=pltpu.HBM)
     dma = pltpu.SemaphoreType.DMA
     table = pltpu.VMEM((6 * rows, width), BF16)
     flat = pltpu.VMEM((rows, width), BF16)
@@ -343,15 +396,16 @@
             flat, flat, flat, flat,
             pltpu.VMEM((rows, width), F32),
             pltpu.VMEM((rows, width), F32),
+            pltpu.VMEM((rows, width), F32),
             flat, flat,
             dma((WEIGHTS + 3,)),
             dma((2, 5 * CHUNKS)), dma((2, 5 * CHUNKS)),
-            dma((3,)), dma((3,)),
+            dma((CHUNKS + 2,)), dma((CHUNKS + 2,)),
             dma((CHUNKS,)), dma((CHUNKS,)),
             dma((CHUNKS,)), dma((CHUNKS,)),
         ],
         compiler_params=pltpu.CompilerParams(
-            collective_id=0, has_side_effects=True, vmem_limit_bytes=48 * 1024 * 1024
+            collective_id=0, has_side_effects=True, vmem_limit_bytes=62 * 1024 * 1024
         ),
     )(
         edge_features, edge_sender.reshape(1, -1), edge_receiver.reshape(1, -1), block_offset,

time: 70.6 us -> 53.1 us (0.75)
  local copies, waits for them, and re-layouts: 16.2 us -> 1.67 us
  Pallas kernels: 53.6 us -> 51.2 us
    unnamed x37 -> x1, local copies, waits for them, and re-layouts: 16.2 us -> 1.67 us
    pallas_call x1, Pallas kernels: 53.6 us -> 51.2 us  [body(): pl.pallas_call(functools.partial(kernel, patches), out_shape=jax.ShapeDty...]
where the time goes in v2:
time: 53.1 us; the launch traced here: 52.9 us
  Pallas kernels  51.2 us (96%)
  local copies, waits for them, and re-layouts  1.67 us (3%)
    pallas_call x1, Pallas kernels, body(): pl.pallas_call(functools.partial(kernel, patches), out_shape=jax.ShapeDty...  51.2 us
    unnamed x1, local copies, waits for them, and re-layouts  1.67 us

profile of v2, /device:TPU:1, one launch (start us, length us, event | category | flops | bytes accessed | tf_op | source)
XLA Modules:
  0.0 52.9 jit_solution(9601242884528934091)
XLA Ops:
  0.0 51.2 %shard_map.226 = bf16[256,512]{1,0:T(8,128)(2,1)} custom-call(bf16[4,1024]{1,0:T(4,128)(2,1)} %feat_ref.1, s32[1,1024]{1,0:T(1,128)} %bitcast.4, s32[1,1024]{1,0:T(1,128)} %bitcast.5, s32[8]{0:T(128)} %offset_ref.1, s32[1,1024]{1,0:T(1,128)} %bitcast.6, s32[1,1024]{1,0:T(1,128)} %bitcast.7, bf16[4,512]{1,0:T(4,128)(2,1)} %fw_ref.1, ...), custom_call_target="tpu_custom_call" | custom-call | tf_op jit(solution)/shard_map/pallas_call | solution.py:377
  51.2 1.7 %copy.26 = bf16[256,512]{1,0:T(8,128)(2,1)} copy(bf16[256,512]{1,0:T(8,128)(2,1)} %shard_map.226) | data formatting | bytes 524288
